TPU v7x, 256 devices: a whole 4x4x8 slice. The times are simulated.
256 devices in a mesh: row: 8 (over x_hi, y), col: 16 (over x_lo, z), rep: 2 (over core).
Axes of the slice: x: 4 (x_hi: 2, x_lo: 2; x = x_hi * 2 + x_lo), y: 4, z: 8, core: 2. Of those that a mesh axis runs over, the one named last changes fastest.
Arguments:
- tokens: bfloat16 [6144, 12288], P(('rep', 'col'), 'row'), parts along dimension 0, may hold values from -6 to 6
- out_grad: bfloat16 [6144, 4096], P(('rep', 'row'), 'col'), parts along dimension 0, may hold values from -0.5 to 0.5
- weight: bfloat16 [24576, 4096], P(('rep', 'row'), 'col'), parts along dimension 0, may hold values from -0.0546875 to 0.0546875
- first_moment: float32 [24576, 4096], P(('rep', 'row'), 'col'), parts along dimension 0, may hold values from -6 to 6
- second_moment: float32 [24576, 4096], P(('rep', 'row'), 'col'), parts along dimension 0, may hold values from 0.5 to 8
Outputs:
- in_grad: bfloat16 [6144, 12288], P(('rep', 'col'), 'row'), parts along dimension 0
- new_weight: bfloat16 [24576, 4096], P(('rep', 'row'), 'col'), parts along dimension 0
- new_first: float32 [24576, 4096], P(('rep', 'row'), 'col'), parts along dimension 0
- new_second: float32 [24576, 4096], P(('rep', 'row'), 'col'), parts along dimension 0
There are 2 independent parts, one for each index of `rep`. A program takes and returns all parts, laid end to end along the dimension named above; each array names one. Nothing has to cross between parts.
All inputs are finite; a program needn't handle non-finite values.
Results may differ from a plain program's by a relative error of at most 0.001.
Values may be sent and summed in bfloat16 or wider, within the bound.
A program may use at most 128 MiB of HBM per device.

v0:
```python
import jax
import jax.numpy as jnp
from jax import lax
from jax.sharding import PartitionSpec as P

ADAM_STEP = 10


def per_device(tokens, out_grad, weight, first_moment, second_moment):
    grad_all = lax.all_gather(out_grad, "row", axis=0, tiled=True)
    match = grad_all
    wgrad = jnp.einsum(
        "td,tf->df",
        lax.all_gather(tokens, "col", axis=0, tiled=True),
        match,
        preferred_element_type=jnp.float32,
    )
    match = grad_all
    summed = lax.psum_scatter(
        jnp.einsum("tf,df->td", match, weight, preferred_element_type=jnp.float32),
        "col",
        scatter_dimension=0,
        tiled=True,
    )
    in_grad = summed.astype(jnp.bfloat16)
    new_first = 0.9 * first_moment + 0.1 * wgrad
    new_second = 0.95 * second_moment + 0.05 * wgrad * wgrad
    first_hat = new_first / (1.0 - 0.9**ADAM_STEP)
    second_hat = new_second / (1.0 - 0.95**ADAM_STEP)
    old = weight.astype(jnp.float32)
    new_weight = (old - 0.001 * first_hat / (jnp.sqrt(second_hat) + 1e-08) - 0.0001 * old).astype(
        jnp.bfloat16
    )
    return (in_grad, new_weight, new_first, new_second)


def solution(mesh):
    placed = (
        P(("rep", "col"), "row"),
        P(("rep", "row"), "col"),
        P(("rep", "row"), "col"),
        P(("rep", "row"), "col"),
        P(("rep", "row"), "col"),
    )
    return jax.shard_map(
        per_device,
        mesh=mesh,
        in_specs=placed,
        out_specs=(
            P(("rep", "col"), "row"),
            P(("rep", "row"), "col"),
            P(("rep", "row"), "col"),
            P(("rep", "row"), "col"),
        ),
        check_vma=False,
    )
```

profile of v0, /device:TPU:4, one launch (start us, length us, event | category | flops | bytes accessed | tf_op | source)
XLA Modules:
  0.0 395.8 jit_solution(5450515752758899545)
XLA Ops:
  7.2 0.0 all-gather.3.cloned.1.call-start
  7.2 0.7 all-gather.3.cloned.1.call-update
  7.9 0.0 all-gather.5.cloned.1.call-start
  7.9 0.7 all-gather.5.cloned.1.call-update
  8.6 0.0 reduce-scatter.2.cloned.1.call-start
  8.7 57.0 %all-gather.3.cloned.1.call-done = bf16[3072,256]{1,0:T(8,128)(2,1)} async-done(((bf16[384,256]{1,0:T(8,128)(2,1)}), bf16[3072,256]{1,0:T(8,128)(2,1)}) %all-gather.3.cloned.1.call-update) | async-done | bytes 1572880 | tf_op jit(solution)/shard_map/all_gather | solution.py:10
  65.7 10.7 %fusion.4 = f32[3072,1536]{1,0:T(8,128)} fusion(bf16[3072,256]{1,0:T(8,128)(2,1)} %all-gather.3.cloned.1.call-done, bf16[1536,256]{1,0:T(8,128)(2,1)} %param.7), kind=kOutput, calls=%fused_computation.7 | convolution fusion | flops 2415919104 | bytes 21233664 | tf_op jit(solution)/shard_map/tf,df->td/dot_general | solution.py:20
  76.4 0.0 copy-start
  76.4 0.0 copy-start.1
  76.4 0.0 reduce-scatter.2.cloned.1.call-update
  76.4 103.6 %all-gather.5.cloned.1.call-done = bf16[3072,1536]{1,0:T(8,128)(2,1)} async-done(((bf16[192,1536]{1,0:T(8,128)(2,1)}), bf16[3072,1536]{1,0:T(8,128)(2,1)}) %all-gather.5.cloned.1.call-update) | async-done | bytes 9437200 | tf_op jit(solution)/shard_map/all_gather | solution.py:14
  180.0 0.0 copy-done
  180.0 0.0 copy-done.1
  180.0 10.3 %fusion.1 = (bf16[1536,256]{1,0:T(8,128)(2,1)}, f32[1536,256]{1,0:T(8,128)}, f32[1536,256]{1,0:T(8,128)}) fusion(bf16[1536,256]{1,0:T(8,128)(2,1)S(1)} %copy-done.1, f32[1536,256]{1,0:T(8,128)} %param.8, f32[1536,256]{1,0:T(8,128)} %param.9, bf16[3072,1536]{1,0:T(8,128)(2,1)} %all-gather.5.cloned.1.call-done, bf16[3072,256]{1,0:T(8,128)(2,1)S(1)} %copy-done), kind=kOutput, calls=%fused_computation.4 | convolution fusion | flops 2422210560 | bytes 18874368 | tf_op jit(solution)/shard_map/td,tf->df/dot_general | solution.py:12
  190.3 196.8 %reduce-scatter.2.cloned.1.call-done = f32[192,1536]{1,0:T(8,128)} async-done(((f32[3072,1536]{1,0:T(8,128)}), f32[192,1536]{1,0:T(8,128)}) %reduce-scatter.2.cloned.1.call-update) | async-done | bytes 1179664 | tf_op jit(solution)/shard_map/reduce_scatter | solution.py:19
  387.1 2.1 convert_element_type.9
Async XLA Ops:
  7.2 58.5 %all-gather.3.cloned.1.call-start = ((), (), s32[]{:S(2)}) async-start(), calls=%async_computation.1 | async-start | bytes 1769472 | tf_op jit(solution)/shard_map/all_gather | solution.py:10
  7.9 172.1 %all-gather.5.cloned.1.call-start = ((), (), s32[]{:S(2)}) async-start(), calls=%async_computation.3 | async-start | bytes 10027008 | tf_op jit(solution)/shard_map/all_gather | solution.py:14
  8.6 378.5 %reduce-scatter.2.cloned.1.call-start = ((), (), s32[]{:S(2)}) async-start(), calls=%async_computation.2 | async-start | bytes 20054016 | tf_op jit(solution)/shard_map/reduce_scatter | solution.py:19
  76.4 103.6 %copy-start = (bf16[3072,256]{1,0:T(8,128)(2,1)S(1)}, bf16[3072,256]{1,0:T(8,128)(2,1)}, u32[]{:S(2)}) copy-start(bf16[3072,256]{1,0:T(8,128)(2,1)} %all-gather.3.cloned.1.call-done) | copy-start | bytes 4718596
  76.4 103.6 %copy-start.1 = (bf16[1536,256]{1,0:T(8,128)(2,1)S(1)}, bf16[1536,256]{1,0:T(8,128)(2,1)}, u32[]{:S(2)}) copy-start(bf16[1536,256]{1,0:T(8,128)(2,1)} %param.7) | copy-start | bytes 2359300
Sparse Core Ops, SparseCore 0:
  10.6 55.0 all-gather.2
  67.4 112.5 all-gather.4
  182.6 204.5 reduce-scatter.1
where the time goes:
time: 397 us; the launch traced here: 396 us
  waiting for transfers between devices  359 us (90%)
  matrix products  21.1 us (5%)
  between operations  13.7 us (3%)
    reduce_scatter x1, waiting for transfers between devices, per_device(): lax.psum_scatter(jnp.einsum('tf,df->td', match, weight, preferred_element...  197 us
    all_gather x1, waiting for transfers between devices, per_device(): lax.all_gather(tokens, 'col', axis=0, tiled=True)  104 us
    all_gather x1, waiting for transfers between devices, per_device(): grad_all = lax.all_gather(out_grad, 'row', axis=0, tiled=True)  57 us
    dot_general x1, matrix products, per_device(): jnp.einsum('tf,df->td', match, weight, preferred_element_type=jnp.float32)  10.7 us
    dot_general x1, matrix products, per_device(): jnp.einsum('td,tf->df', lax.all_gather(tokens, 'col', axis=0, tiled=True)...  10.3 us
  transfers between devices with their start and end apart: 3, of which 3 were waited for; matrix products, arithmetic and copies ran while one was open for 5% of the time, Pallas kernels for 0%

commit v1 on v0

v1 whole, which is shorter than its diff:
```python
import functools

import jax
import jax.numpy as jnp
from jax import lax
from jax.experimental import pallas as pl
from jax.experimental.pallas import tpu as pltpu
from jax.sharding import PartitionSpec as P

ADAM_STEP = 10
MESH = pl.DeviceIdType.MESH
XH, XL, NY, NZ = 2, 2, 4, 8
CHUNK = 384


def kernel(
    tokens, og, weight, wgrad_out, in_grad_out,
    tk, wg, ogy, ogw, ogi, part, part_in, quota, quota_in, in_grad,
    ring_send, ring_recv, y_send, y_recv, w_send, w_recv, z_send, z_recv,
    h_send, h_recv, b_send, b_recv, x_send, x_recv, local,
):
    tb, d = tokens.shape
    ob, f = og.shape
    n_chunks = d // CHUNK
    n_items = 2 * n_chunks
    quarter = tb // NY
    half_t = NZ * tb

    r, c = lax.axis_index("row"), lax.axis_index("col")
    xh, y = r // NY, lax.rem(r, NY)
    xl, z = c // NZ, lax.rem(c, NZ)

    def dev(xh_, y_, xl_, z_):
        return {"row": xh_ * NY + y_, "col": xl_ * NZ + z_}

    def remote(src, dst, s, rcv, to):
        return pltpu.make_async_remote_copy(
            src_ref=src, dst_ref=dst, send_sem=s, recv_sem=rcv, device_id=to, device_id_type=MESH
        )

    own = [
        pltpu.make_async_copy(tokens, tk.at[z], local.at[0]),
        pltpu.make_async_copy(weight, wg.at[z], local.at[1]),
        pltpu.make_async_copy(og, ogy.at[pl.ds(y * ob, ob)], local.at[2]),
    ]
    for o in own:
        o.start()

    barrier = pltpu.get_barrier_semaphore()
    peers = [dev(xh, lax.rem(y + k, NY), xl, z) for k in range(1, NY)]
    peers += [dev(xh, y, xl, lax.rem(z + k, NZ)) for k in range(1, NZ)]
    peers += [dev(1 - xh, y, xl, z), dev(xh, y, 1 - xl, z), dev(1 - xh, y, 1 - xl, z)]
    for p in peers:
        pl.semaphore_signal(barrier, inc=1, device_id=p, device_id_type=MESH)
    pl.semaphore_wait(barrier, len(peers))

    y_copies = []
    for k in range(1, NY):
        y_copies.append(
            remote(og, ogy.at[pl.ds(y * ob, ob)], y_send.at[k - 1], y_recv.at[k - 1], dev(xh, lax.rem(y + k, NY), xl, z))
        )
        y_copies[-1].start()

    right, left = lax.rem(z + 1, NZ), lax.rem(z + NZ - 1, NZ)

    def piece(item, src_z, half):
        if item < n_chunks:
            rows = pl.ds(0, tb) if half is None else pl.ds(half * (tb // 2), tb // 2)
            return tk.at[src_z, rows, pl.ds(item * CHUNK, CHUNK)]
        d0 = (item - n_chunks) * CHUNK
        rows = pl.ds(d0, CHUNK) if half is None else pl.ds(d0 + half * (CHUNK // 2), CHUNK // 2)
        return wg.at[src_z, rows]

    def ring_copy(item, way, hop):
        half = way if hop == NZ // 2 else None
        step = hop - 1
        src_z = lax.rem(z + (NZ - step if way == 0 else step), NZ)
        ref = piece(item, src_z, half)
        if hop == 1:
            if item < n_chunks:
                src = tokens.at[:, pl.ds(item * CHUNK, CHUNK)]
            else:
                src = weight.at[pl.ds((item - n_chunks) * CHUNK, CHUNK)]
        else:
            src = ref
        to = right if way == 0 else left
        return remote(src, ref, ring_send.at[item, way, step], ring_recv.at[item, way, step], dev(xh, y, xl, to))

    def ring_arrival(item, way, hop):
        half = way if hop == NZ // 2 else None
        src_z = lax.rem(z + (NZ - hop if way == 0 else hop), NZ)
        ref = piece(item, src_z, half)
        return remote(ref, ref, ring_send.at[item, way, hop - 1], ring_recv.at[item, way, hop - 1], dev(xh, y, xl, right))

    ring_copies = []

    def ring_start(item, hop):
        for way in (0, 1):
            copy = ring_copy(item, way, hop)
            copy.start()
            ring_copies.append(copy)

    same = xh == xl

    def w_copy(k):
        return remote(ogy, ogw.at[xl], w_send.at[k], w_recv.at[xl], dev(k, y, xh, z))

    def w_arrival(j):
        return remote(ogy, ogw.at[j], w_send.at[j], w_recv.at[j], dev(xh, y, 1 - xl, z))

    def w_local():
        return pltpu.make_async_copy(ogy, ogw.at[xl], local.at[3])

    def w_start():
        for k in range(XH):
            @pl.when(jnp.logical_or(k != xh, jnp.logical_not(same)))
            def _():
                w_copy(k).start()

        @pl.when(same)
        def _():
            w_local().start()

    def w_wait():
        for j in range(XL):
            @pl.when(jnp.logical_or(j != xl, jnp.logical_not(same)))
            def _():
                w_arrival(j).wait_recv()

        @pl.when(same)
        def _():
            w_local().wait()

    def w_wait_send():
        for k in range(XH):
            @pl.when(jnp.logical_or(k != xh, jnp.logical_not(same)))
            def _():
                w_copy(k).wait_send()

    def strip(h, y_):
        return ogi.at[:, h, pl.ds(y_ * quarter, quarter)]

    def z_copy(k):
        to = lax.rem(z + k, NZ)
        src = ogy.at[pl.ds(to * tb + y * quarter, quarter)]
        return remote(src, ogi.at[z, xh, pl.ds(y * quarter, quarter)], z_send.at[k - 1], z_recv.at[k - 1], dev(xh, y, xl, to))

    def z_arrival(k):
        at = lax.rem(z + NZ - k, NZ)
        ref = ogi.at[at, xh, pl.ds(y * quarter, quarter)]
        return remote(ref, ref, z_send.at[k - 1], z_recv.at[k - 1], dev(xh, y, xl, at))

    z_local = pltpu.make_async_copy(
        ogy.at[pl.ds(z * tb + y * quarter, quarter)], ogi.at[z, xh, pl.ds(y * quarter, quarter)], local.at[4]
    )
    h_copy = remote(strip(xh, y), strip(xh, y), h_send, h_recv, dev(1 - xh, y, xl, z))
    h_arrival = remote(strip(1 - xh, y), strip(1 - xh, y), h_send, h_recv, dev(1 - xh, y, xl, z))

    def b_copy(which, k):
        h = xh if which == 0 else 1 - xh
        return remote(strip(h, y), strip(h, y), b_send.at[which, k - 1], b_recv.at[which, k - 1], dev(xh, lax.rem(y + k, NY), xl, z))

    def b_arrival(which, k):
        h = xh if which == 0 else 1 - xh
        ref = strip(h, lax.rem(y + NY - k, NY))
        return remote(ref, ref, b_send.at[which, k - 1], b_recv.at[which, k - 1], dev(xh, lax.rem(y + k, NY), xl, z))

    def x_copy(item):
        d0 = (item % n_chunks) * CHUNK
        if item < n_chunks:
            src, dst = part.at[1 - xl, pl.ds(d0, CHUNK)], part_in.at[pl.ds(d0, CHUNK)]
        else:
            src, dst = quota.at[1 - xl, :, pl.ds(d0, CHUNK)], quota_in.at[:, pl.ds(d0, CHUNK)]
        return remote(src, dst, x_send.at[item], x_recv.at[item], dev(xh, y, 1 - xl, z))

    def multiply(item):
        d0 = (item % n_chunks) * CHUNK
        if item < n_chunks:
            def body(i, _):
                cols = pl.ds(pl.multiple_of(d0 + i * 128, 128), 128)
                a = tk[:, :, cols].reshape(half_t, 128)
                for k in range(XL):
                    part[k, cols] = lax.dot_general(
                        a, ogw[k], (((0,), (0,)), ((), ())), preferred_element_type=jnp.float32
                    )
                return 0

            lax.fori_loop(0, CHUNK // 128, body, 0)
        else:
            def body(i, _):
                k = i
                total = jnp.zeros((tb, CHUNK), jnp.float32)
                for s in range(NZ):
                    total += lax.dot_general(
                        ogi[s, k], wg[s, pl.ds(d0, CHUNK)], (((1,), (1,)), ((), ())), preferred_element_type=jnp.float32
                    )
                quota[k, :, pl.ds(d0, CHUNK)] = total
                return 0

            lax.fori_loop(0, XL, body, 0)

    outs = []

    def finish(item):
        d0 = (item % n_chunks) * CHUNK
        x_copy(item).wait_recv()
        if item < n_chunks:
            part[xl, pl.ds(d0, CHUNK)] = part[xl, pl.ds(d0, CHUNK)] + part_in[pl.ds(d0, CHUNK)]
            out = pltpu.make_async_copy(part.at[xl, pl.ds(d0, CHUNK)], wgrad_out.at[pl.ds(d0, CHUNK)], local.at[5 + item])
        else:
            cols = pl.ds(d0, CHUNK)
            in_grad[:, cols] = (quota[xl, :, cols] + quota_in[:, cols]).astype(in_grad.dtype)
            out = pltpu.make_async_copy(in_grad.at[:, cols], in_grad_out.at[:, cols], local.at[5 + item])
        out.start()
        outs.append(out)

    hops = NZ // 2
    ring_start(0, 1)
    ring_start(1, 1)
    for step in range(n_items + hops - 1):
        for hop in range(hops, 0, -1):
            item = step - (hop - 1)
            if 0 <= item < n_items:
                for way in (0, 1):
                    ring_arrival(item, way, hop).wait_recv()
                if hop < hops:
                    ring_start(item, hop + 1)
        if step + 2 < n_items:
            ring_start(step + 2, 1)
        if step == 0:
            own[2].wait()
            for k in range(1, NY):
                src = ogy.at[pl.ds(lax.rem(y + NY - k, NY) * ob, ob)]
                remote(src, src, y_send.at[k - 1], y_recv.at[k - 1], dev(xh, lax.rem(y + k, NY), xl, z)).wait_recv()
            w_start()
            for k in range(1, NZ):
                z_copy(k).start()
            z_local.start()
        if step == 1:
            z_local.wait()
            for k in range(1, NZ):
                z_arrival(k).wait_recv()
            h_copy.start()
            for k in range(1, NY):
                b_copy(0, k).start()
        if step == 2:
            h_arrival.wait_recv()
            for k in range(1, NY):
                b_copy(1, k).start()
            own[0].wait()
            own[1].wait()
        done = step - (hops - 1)
        if done == 0:
            w_wait()
        if done == 2:
            for which in (0, 1):
                for k in range(1, NY):
                    b_arrival(which, k).wait_recv()
        if done >= 0:
            multiply(done)
            x_copy(done).start()
            if done >= 2:
                finish(done - 2)
    finish(n_items - 2)
    finish(n_items - 1)

    for copy in y_copies + ring_copies:
        copy.wait_send()
    w_wait_send()
    for k in range(1, NZ):
        z_copy(k).wait_send()
    h_copy.wait_send()
    for which in (0, 1):
        for k in range(1, NY):
            b_copy(which, k).wait_send()
    for item in range(n_items):
        x_copy(item).wait_send()
    for out in outs:
        out.wait()


def products(tokens, out_grad, weight):
    tb, d = tokens.shape
    ob, f = out_grad.shape
    n_items = 2 * (d // CHUNK)
    dma = pltpu.SemaphoreType.DMA
    flops = 4 * d * f * ob * XH * NY
    return pl.pallas_call(
        kernel,
        out_shape=(
            jax.ShapeDtypeStruct((d, f), jnp.float32),
            jax.ShapeDtypeStruct((tb, d), jnp.bfloat16),
        ),
        in_specs=[pl.BlockSpec(memory_space=pl.ANY)] * 3,
        out_specs=[pl.BlockSpec(memory_space=pl.ANY)] * 2,
        scratch_shapes=[
            pltpu.VMEM((NZ, tb, d), jnp.bfloat16),
            pltpu.VMEM((NZ, d, f), jnp.bfloat16),
            pltpu.VMEM((NY * ob, f), jnp.bfloat16),
            pltpu.VMEM((XL, NY * ob, f), jnp.bfloat16),
            pltpu.VMEM((NZ, XH, tb, f), jnp.bfloat16),
            pltpu.VMEM((XL, d, f), jnp.float32),
            pltpu.VMEM((d, f), jnp.float32),
            pltpu.VMEM((XL, tb, d), jnp.float32),
            pltpu.VMEM((tb, d), jnp.float32),
            pltpu.VMEM((tb, d), jnp.bfloat16),
            dma((n_items, 2, NZ // 2)),
            dma((n_items, 2, NZ // 2)),
            dma((NY - 1,)),
            dma((NY - 1,)),
            dma((XH,)),
            dma((XL,)),
            dma((NZ - 1,)),
            dma((NZ - 1,)),
            dma,
            dma,
            dma((2, NY - 1)),
            dma((2, NY - 1)),
            dma((n_items,)),
            dma((n_items,)),
            dma((5 + n_items,)),
        ],
        compiler_params=pltpu.CompilerParams(
            collective_id=0, has_side_effects=True, vmem_limit_bytes=48 * 2**20
        ),
        cost_estimate=pl.CostEstimate(flops=flops, bytes_accessed=8 * 2**20, transcendentals=0),
    )(tokens, out_grad, weight)


def per_device(tokens, out_grad, weight, first_moment, second_moment):
    wgrad, in_grad = products(tokens, out_grad, weight)
    new_first = 0.9 * first_moment + 0.1 * wgrad
    new_second = 0.95 * second_moment + 0.05 * wgrad * wgrad
    first_hat = new_first / (1.0 - 0.9**ADAM_STEP)
    second_hat = new_second / (1.0 - 0.95**ADAM_STEP)
    old = weight.astype(jnp.float32)
    new_weight = (old - 0.001 * first_hat / (jnp.sqrt(second_hat) + 1e-08) - 0.0001 * old).astype(
        jnp.bfloat16
    )
    return (in_grad, new_weight, new_first, new_second)


def solution(mesh):
    placed = (
        P(("rep", "col"), "row"),
        P(("rep", "row"), "col"),
        P(("rep", "row"), "col"),
        P(("rep", "row"), "col"),
        P(("rep", "row"), "col"),
    )
    return jax.shard_map(
        per_device,
        mesh=mesh,
        in_specs=placed,
        out_specs=(
            P(("rep", "col"), "row"),
            P(("rep", "row"), "col"),
            P(("rep", "row"), "col"),
            P(("rep", "row"), "col"),
        ),
        check_vma=False,
    )
```

time: 397 us -> 141 us (0.36)
  waiting for transfers between devices: 359 us -> 0 us
  Pallas kernels: 0 us -> 132 us
  matrix products: 21.1 us -> 0 us
  between operations: 13.7 us -> 0.67 us
    reduce_scatter x1 -> x0, waiting for transfers between devices: 197 us -> none  [per_device(): lax.psum_scatter(jnp.einsum('tf,df->td', match, weight, preferred_element...]
    all_gather x2 -> x0, waiting for transfers between devices: 161 us -> none  [the longest x1 104 us: per_device(): lax.all_gather(tokens, 'col', axis=0, tiled=True)]
    pallas_call x0 -> x1, Pallas kernels: none -> 132 us  [products(): pl.pallas_call(kernel, out_shape=(jax.ShapeDtypeStruct((d, f), jnp.float3...]
    dot_general x2 -> x0, matrix products: 21.1 us -> none  [the longest x1 10.7 us: per_device(): jnp.einsum('tf,df->td', match, weight, preferred_element_type=jnp.float32)]
  transfers between devices with their start and end apart: 3 -> 0, of which waited for: 3 -> 0; matrix products, arithmetic and copies ran while one was open for 5% -> 0% of each run, Pallas kernels for 0% -> 0%
where the time goes in v1:
time: 141 us; the launch traced here: 140 us
  Pallas kernels  132 us (94%)
  local copies, waits for them, and re-layouts  3.94 us (3%)
  other arithmetic  2.83 us (2%)
    pallas_call x1, Pallas kernels, products(): pl.pallas_call(kernel, out_shape=(jax.ShapeDtypeStruct((d, f), jnp.float3...  132 us
    unnamed x11, local copies, waits for them, and re-layouts  3.94 us
    convert_element_type x1, other arithmetic, per_device(): (old - 0.001 * first_hat / (jnp.sqrt(second_hat) + 1e-08) - 0.0001 * old)...  2.83 us

profile of v1, /device:TPU:4, one launch (start us, length us, event | category | flops | bytes accessed | tf_op | source)
XLA Modules:
  0.0 139.9 jit_solution(706969439665107344)
XLA Ops:
  0.6 0.0 copy-start
  0.6 1.1 copy-done
  1.8 0.0 copy-start.1
  1.8 1.1 copy-done.1
  2.8 0.0 copy-start.2
  2.8 0.9 copy-done.2
  3.8 0.0 copy-start.3
  3.8 0.0 copy-start.4
  3.8 132.5 %shard_map.84 = (f32[1536,256]{1,0:T(8,128)S(1)}, bf16[192,1536]{1,0:T(8,128)(2,1)S(1)}) custom-call(bf16[192,1536]{1,0:T(8,128)(2,1)S(1)} %copy-done.1, bf16[384,256]{1,0:T(8,128)(2,1)S(1)} %copy-done.2, bf16[1536,256]{1,0:T(8,128)(2,1)S(1)} %copy-done), custom_call_target="tpu_custom_call" | custom-call | flops 4831838208 | bytes 8388608 | tf_op jit(solution)/shard_map/pallas_call | solution.py:288
  136.2 0.0 copy-done.3
  136.2 0.0 copy-done.4
  136.3 2.8 %fusion.1 = (bf16[1536,256]{1,0:T(8,128)(2,1)}, f32[1536,256]{1,0:T(8,128)}, f32[1536,256]{1,0:T(8,128)}) fusion(bf16[1536,256]{1,0:T(8,128)(2,1)S(1)} %copy-done, f32[1536,256]{1,0:T(8,128)S(1)} %get-tuple-element.7, f32[1536,256]{1,0:T(8,128)S(1)} %copy-done.3, f32[1536,256]{1,0:T(8,128)S(1)} %copy-done.4), kind=kLoop, calls=%fused_computation.4 | loop fusion | flops 6291456 | bytes 9437184 | tf_op jit(solution)/shard_map/convert_element_type | solution.py:337
  139.1 0.8 copy.10
Async XLA Ops:
  0.6 1.1 copy-start
  1.8 1.1 copy-start.1
  2.8 0.9 copy-start.2
  3.8 132.5 %copy-start.3 = (f32[1536,256]{1,0:T(8,128)S(1)}, f32[1536,256]{1,0:T(8,128)}, u32[]{:S(2)}) copy-start(f32[1536,256]{1,0:T(8,128)} %param.8) | copy-start | bytes 4718596
  3.8 132.5 %copy-start.4 = (f32[1536,256]{1,0:T(8,128)S(1)}, f32[1536,256]{1,0:T(8,128)}, u32[]{:S(2)}) copy-start(f32[1536,256]{1,0:T(8,128)} %param.9) | copy-start | bytes 4718596

commit v2 on v1

--- a/solution.py
+++ b/solution.py
@@ -10,7 +10,30 @@
 ADAM_STEP = 10
 MESH = pl.DeviceIdType.MESH
 XH, XL, NY, NZ = 2, 2, 4, 8
-CHUNK = 384
+LOOK = 4
+TOKEN_CHUNKS = (384, 384, 384, 384)
+WEIGHT_CHUNKS = (384, 384, 384, 256, 128)
+LAST = 128
+PACE = 1
+DRAIN = 0
+SETTLE = 2
+STAGES = (0, 1, 2)
+
+
+def chunks():
+    items = []
+    for widths in (TOKEN_CHUNKS, WEIGHT_CHUNKS):
+        first = 0
+        for width in widths:
+            items.append((first, width))
+            first += width
+    return items
+
+
+def parts_of(items):
+    parts = [(item, first, width) for item, (first, width) in enumerate(items[:-1])]
+    first, width = items[-1]
+    return parts + [(len(items) - 1, first + at, LAST) for at in range(0, width, LAST)]
 
 
 def kernel(
@@ -21,8 +44,9 @@
 ):
     tb, d = tokens.shape
     ob, f = og.shape
-    n_chunks = d // CHUNK
-    n_items = 2 * n_chunks
+    n_chunks, items = len(TOKEN_CHUNKS), chunks()
+    n_items = len(items)
+    prods = parts_of(items)
     quarter = tb // NY
     half_t = NZ * tb
 
@@ -64,11 +88,11 @@
     right, left = lax.rem(z + 1, NZ), lax.rem(z + NZ - 1, NZ)
 
     def piece(item, src_z, half):
+        d0, width = items[item]
         if item < n_chunks:
             rows = pl.ds(0, tb) if half is None else pl.ds(half * (tb // 2), tb // 2)
-            return tk.at[src_z, rows, pl.ds(item * CHUNK, CHUNK)]
-        d0 = (item - n_chunks) * CHUNK
-        rows = pl.ds(d0, CHUNK) if half is None else pl.ds(d0 + half * (CHUNK // 2), CHUNK // 2)
+            return tk.at[src_z, rows, pl.ds(d0, width)]
+        rows = pl.ds(d0, width) if half is None else pl.ds(d0 + half * (width // 2), width // 2)
         return wg.at[src_z, rows]
 
     def ring_copy(item, way, hop):
@@ -76,13 +100,7 @@
         step = hop - 1
         src_z = lax.rem(z + (NZ - step if way == 0 else step), NZ)
         ref = piece(item, src_z, half)
-        if hop == 1:
-            if item < n_chunks:
-                src = tokens.at[:, pl.ds(item * CHUNK, CHUNK)]
-            else:
-                src = weight.at[pl.ds((item - n_chunks) * CHUNK, CHUNK)]
-        else:
-            src = ref
+        src = ref
         to = right if way == 0 else left
         return remote(src, ref, ring_send.at[item, way, step], ring_recv.at[item, way, step], dev(xh, y, xl, to))
 
@@ -92,10 +110,11 @@
         ref = piece(item, src_z, half)
         return remote(ref, ref, ring_send.at[item, way, hop - 1], ring_recv.at[item, way, hop - 1], dev(xh, y, xl, right))
 
+    own[0].wait()
     ring_copies = []
 
-    def ring_start(item, hop):
-        for way in (0, 1):
+    def ring_start(item, hop, ways=(0, 1)):
+        for way in ways:
             copy = ring_copy(item, way, hop)
             copy.start()
             ring_copies.append(copy)
@@ -165,16 +184,16 @@
         ref = strip(h, lax.rem(y + NY - k, NY))
         return remote(ref, ref, b_send.at[which, k - 1], b_recv.at[which, k - 1], dev(xh, lax.rem(y + k, NY), xl, z))
 
-    def x_copy(item):
-        d0 = (item % n_chunks) * CHUNK
+    def x_copy(at):
+        item, d0, width = prods[at]
         if item < n_chunks:
-            src, dst = part.at[1 - xl, pl.ds(d0, CHUNK)], part_in.at[pl.ds(d0, CHUNK)]
+            src, dst = part.at[1 - xl, pl.ds(d0, width)], part_in.at[pl.ds(d0, width)]
         else:
-            src, dst = quota.at[1 - xl, :, pl.ds(d0, CHUNK)], quota_in.at[:, pl.ds(d0, CHUNK)]
-        return remote(src, dst, x_send.at[item], x_recv.at[item], dev(xh, y, 1 - xl, z))
-
-    def multiply(item):
-        d0 = (item % n_chunks) * CHUNK
+            src, dst = quota.at[1 - xl, :, pl.ds(d0, width)], quota_in.at[:, pl.ds(d0, width)]
+        return remote(src, dst, x_send.at[at], x_recv.at[at], dev(xh, y, 1 - xl, z))
+
+    def multiply(at):
+        item, d0, width = prods[at]
         if item < n_chunks:
             def body(i, _):
                 cols = pl.ds(pl.multiple_of(d0 + i * 128, 128), 128)
@@ -185,49 +204,56 @@
                     )
                 return 0
 
-            lax.fori_loop(0, CHUNK // 128, body, 0)
+            lax.fori_loop(0, width // 128, body, 0)
         else:
             def body(i, _):
                 k = i
-                total = jnp.zeros((tb, CHUNK), jnp.float32)
+                total = jnp.zeros((tb, width), jnp.float32)
                 for s in range(NZ):
                     total += lax.dot_general(
-                        ogi[s, k], wg[s, pl.ds(d0, CHUNK)], (((1,), (1,)), ((), ())), preferred_element_type=jnp.float32
+                        ogi[s, k], wg[s, pl.ds(d0, width)], (((1,), (1,)), ((), ())), preferred_element_type=jnp.float32
                     )
-                quota[k, :, pl.ds(d0, CHUNK)] = total
+                quota[k, :, pl.ds(d0, width)] = total
                 return 0
 
             lax.fori_loop(0, XL, body, 0)
 
     outs = []
 
-    def finish(item):
-        d0 = (item % n_chunks) * CHUNK
-        x_copy(item).wait_recv()
+    def finish(at):
+        item, d0, width = prods[at]
+        x_copy(at).wait_recv()
         if item < n_chunks:
-            part[xl, pl.ds(d0, CHUNK)] = part[xl, pl.ds(d0, CHUNK)] + part_in[pl.ds(d0, CHUNK)]
-            out = pltpu.make_async_copy(part.at[xl, pl.ds(d0, CHUNK)], wgrad_out.at[pl.ds(d0, CHUNK)], local.at[5 + item])
+            part[xl, pl.ds(d0, width)] = part[xl, pl.ds(d0, width)] + part_in[pl.ds(d0, width)]
+            out = pltpu.make_async_copy(part.at[xl, pl.ds(d0, width)], wgrad_out.at[pl.ds(d0, width)], local.at[5 + at])
         else:
-            cols = pl.ds(d0, CHUNK)
+            cols = pl.ds(d0, width)
             in_grad[:, cols] = (quota[xl, :, cols] + quota_in[:, cols]).astype(in_grad.dtype)
-            out = pltpu.make_async_copy(in_grad.at[:, cols], in_grad_out.at[:, cols], local.at[5 + item])
+            out = pltpu.make_async_copy(in_grad.at[:, cols], in_grad_out.at[:, cols], local.at[5 + at])
         out.start()
         outs.append(out)
 
     hops = NZ // 2
-    ring_start(0, 1)
-    ring_start(1, 1)
-    for step in range(n_items + hops - 1):
+    waiting = []
+    next_product = 0
+    for item in range(LOOK):
+        ring_start(item, 1)
+
+    def due(item, hop):
+        return min(item + PACE * (hop - 1), n_items - 1 + DRAIN + hop - 1)
+
+    for step in range(due(n_items - 1, hops) + 1):
         for hop in range(hops, 0, -1):
-            item = step - (hop - 1)
-            if 0 <= item < n_items:
+            for item in [i for i in range(n_items) if due(i, hop) == step]:
                 for way in (0, 1):
                     ring_arrival(item, way, hop).wait_recv()
-                if hop < hops:
-                    ring_start(item, hop + 1)
-        if step + 2 < n_items:
-            ring_start(step + 2, 1)
-        if step == 0:
+                    if hop < hops:
+                        ring_start(item, hop + 1, (way,))
+        if step + LOOK < n_items:
+            if step + LOOK == n_chunks:
+                own[1].wait()
+            ring_start(step + LOOK, 1)
+        if step == STAGES[0]:
             own[2].wait()
             for k in range(1, NY):
                 src = ogy.at[pl.ds(lax.rem(y + NY - k, NY) * ob, ob)]
@@ -236,33 +262,32 @@
             for k in range(1, NZ):
                 z_copy(k).start()
             z_local.start()
-        if step == 1:
+        if step == STAGES[1]:
             z_local.wait()
             for k in range(1, NZ):
                 z_arrival(k).wait_recv()
             h_copy.start()
             for k in range(1, NY):
                 b_copy(0, k).start()
-        if step == 2:
+        if step == STAGES[2]:
             h_arrival.wait_recv()
             for k in range(1, NY):
                 b_copy(1, k).start()
-            own[0].wait()
-            own[1].wait()
-        done = step - (hops - 1)
-        if done == 0:
-            w_wait()
-        if done == 2:
-            for which in (0, 1):
-                for k in range(1, NY):
-                    b_arrival(which, k).wait_recv()
-        if done >= 0:
-            multiply(done)
-            x_copy(done).start()
-            if done >= 2:
-                finish(done - 2)
-    finish(n_items - 2)
-    finish(n_items - 1)
+        while next_product < len(prods) and due(prods[next_product][0], hops) <= step:
+            if next_product == 0:
+                w_wait()
+            if next_product == n_chunks:
+                for which in (0, 1):
+                    for k in range(1, NY):
+                        b_arrival(which, k).wait_recv()
+            multiply(next_product)
+            x_copy(next_product).start()
+            waiting.append((step, next_product))
+            next_product += 1
+        while waiting and waiting[0][0] <= step - SETTLE:
+            finish(waiting.pop(0)[1])
+    for _, item in waiting:
+        finish(item)
 
     for copy in y_copies + ring_copies:
         copy.wait_send()
@@ -273,8 +298,8 @@
     for which in (0, 1):
         for k in range(1, NY):
             b_copy(which, k).wait_send()
-    for item in range(n_items):
-        x_copy(item).wait_send()
+    for at in range(len(prods)):
+        x_copy(at).wait_send()
     for out in outs:
         out.wait()
 
@@ -282,7 +307,8 @@
 def products(tokens, out_grad, weight):
     tb, d = tokens.shape
     ob, f = out_grad.shape
-    n_items = 2 * (d // CHUNK)
+    items = chunks()
+    n_items, n_prods = len(items), len(parts_of(items))
     dma = pltpu.SemaphoreType.DMA
     flops = 4 * d * f * ob * XH * NY
     return pl.pallas_call(
@@ -291,7 +317,7 @@
             jax.ShapeDtypeStruct((d, f), jnp.float32),
             jax.ShapeDtypeStruct((tb, d), jnp.bfloat16),
         ),
-        in_specs=[pl.BlockSpec(memory_space=pl.ANY)] * 3,
+        in_specs=[pl.BlockSpec(memory_space=pltpu.HBM)] * 3,
         out_specs=[pl.BlockSpec(memory_space=pl.ANY)] * 2,
         scratch_shapes=[
             pltpu.VMEM((NZ, tb, d), jnp.bfloat16),
@@ -316,12 +342,12 @@
             dma,
             dma((2, NY - 1)),
             dma((2, NY - 1)),
-            dma((n_items,)),
-            dma((n_items,)),
-            dma((5 + n_items,)),
+            dma((n_prods,)),
+            dma((n_prods,)),
+            dma((5 + n_prods,)),
         ],
         compiler_params=pltpu.CompilerParams(
-            collective_id=0, has_side_effects=True, vmem_limit_bytes=48 * 2**20
+            collective_id=0, has_side_effects=True, vmem_limit_bytes=60 * 2**20
         ),
         cost_estimate=pl.CostEstimate(flops=flops, bytes_accessed=8 * 2**20, transcendentals=0),
     )(tokens, out_grad, weight)

time: 141 us -> 138 us (0.979)
  local copies, waits for them, and re-layouts: 3.94 us -> 0.83 us
  other arithmetic: 2.83 us -> 4.28 us
    unnamed x11 -> x9, local copies, waits for them, and re-layouts: 3.94 us -> 0.83 us
    convert_element_type x1, other arithmetic: 2.83 us -> 4.28 us  [per_device(): (old - 0.001 * first_hat / (jnp.sqrt(second_hat) + 1e-08) - 0.0001 * old)...]
where the time goes in v2:
time: 138 us
  Pallas kernels  132 us (96%)
  other arithmetic  4.28 us (3%)
    pallas_call x1, Pallas kernels, products(): pl.pallas_call(kernel, out_shape=(jax.ShapeDtypeStruct((d, f), jnp.float3...  132 us
    convert_element_type x1, other arithmetic, per_device(): (old - 0.001 * first_hat / (jnp.sqrt(second_hat) + 1e-08) - 0.0001 * old)...  4.28 us

profile of v2, /device:TPU:4, one launch (start us, length us, event | category | flops | bytes accessed | tf_op | source)
XLA Modules:
  0.0 137.7 jit_solution(17479083013062391398)
XLA Ops:
  0.6 0.0 copy-start.2
  0.6 0.0 copy-start.1
  0.7 0.0 copy-start
  0.7 131.9 %shard_map.84 = (f32[1536,256]{1,0:T(8,128)}, bf16[192,1536]{1,0:T(8,128)(2,1)}) custom-call(bf16[192,1536]{1,0:T(8,128)(2,1)} %tokens.1, bf16[384,256]{1,0:T(8,128)(2,1)} %og.1, bf16[1536,256]{1,0:T(8,128)(2,1)} %weight.1), custom_call_target="tpu_custom_call" | custom-call | flops 4831838208 | bytes 8388608 | tf_op jit(solution)/shard_map/pallas_call | solution.py:314
  132.5 0.0 copy-done.2
  132.6 0.0 copy-done.1
  132.6 0.0 copy-done
  132.6 0.0 copy-start.3
  132.6 4.3 %fusion.1 = (bf16[1536,256]{1,0:T(8,128)(2,1)}, f32[1536,256]{1,0:T(8,128)}, f32[1536,256]{1,0:T(8,128)}) fusion(bf16[1536,256]{1,0:T(8,128)(2,1)S(1)} %copy-done.2, f32[1536,256]{1,0:T(8,128)} %get-tuple-element.7, f32[1536,256]{1,0:T(8,128)S(1)} %copy-done, f32[1536,256]{1,0:T(8,128)S(1)} %copy-done.1), kind=kLoop, calls=%fused_computation.4 | loop fusion | flops 6291456 | bytes 9437184 | tf_op jit(solution)/shard_map/convert_element_type | solution.py:363
  136.9 0.0 copy-done.3
  136.9 0.8 copy.10
Async XLA Ops:
  0.6 131.9 %copy-start.2 = (bf16[1536,256]{1,0:T(8,128)(2,1)S(1)}, bf16[1536,256]{1,0:T(8,128)(2,1)}, u32[]{:S(2)}) copy-start(bf16[1536,256]{1,0:T(8,128)(2,1)} %weight.1) | copy-start | bytes 2359300
  0.6 131.9 %copy-start.1 = (f32[1536,256]{1,0:T(8,128)S(1)}, f32[1536,256]{1,0:T(8,128)}, u32[]{:S(2)}) copy-start(f32[1536,256]{1,0:T(8,128)} %param.9) | copy-start | bytes 4718596
  0.7 131.9 %copy-start = (f32[1536,256]{1,0:T(8,128)S(1)}, f32[1536,256]{1,0:T(8,128)}, u32[]{:S(2)}) copy-start(f32[1536,256]{1,0:T(8,128)} %param.8) | copy-start | bytes 4718596
  132.6 4.3 %copy-start.3 = (bf16[192,1536]{1,0:T(8,128)(2,1)S(1)}, bf16[192,1536]{1,0:T(8,128)(2,1)}, u32[]{:S(2)}) copy-start(bf16[192,1536]{1,0:T(8,128)(2,1)} %get-tuple-element.15) | copy-start | bytes 1769476

commit v3 on v2

--- a/solution.py
+++ b/solution.py
@@ -39,7 +39,7 @@
 def kernel(
     tokens, og, weight, wgrad_out, in_grad_out,
     tk, wg, ogy, ogw, ogi, part, part_in, quota, quota_in, in_grad,
-    ring_send, ring_recv, y_send, y_recv, w_send, w_recv, z_send, z_recv,
+    ring_send, ring_recv, y_send, y_recv, w_send, w_recv, v_send, v_recv, z_send, z_recv,
     h_send, h_recv, b_send, b_recv, x_send, x_recv, local,
 ):
     tb, d = tokens.shape
@@ -122,13 +122,14 @@
     same = xh == xl
 
     def w_copy(k):
-        return remote(ogy, ogw.at[xl], w_send.at[k], w_recv.at[xl], dev(k, y, xh, z))
+        return remote(og, ogw.at[xl, pl.ds(y * ob, ob)], w_send.at[k], w_recv.at[xl], dev(k, y, xh, z))
 
     def w_arrival(j):
-        return remote(ogy, ogw.at[j], w_send.at[j], w_recv.at[j], dev(xh, y, 1 - xl, z))
+        ref = ogw.at[j, pl.ds(y * ob, ob)]
+        return remote(ref, ref, w_send.at[j], w_recv.at[j], dev(xh, y, 1 - xl, z))
 
     def w_local():
-        return pltpu.make_async_copy(ogy, ogw.at[xl], local.at[3])
+        return pltpu.make_async_copy(og, ogw.at[xl, pl.ds(y * ob, ob)], local.at[3])
 
     def w_start():
         for k in range(XH):
@@ -155,6 +156,14 @@
             @pl.when(jnp.logical_or(k != xh, jnp.logical_not(same)))
             def _():
                 w_copy(k).wait_send()
+
+    def v_copy(k):
+        ref = ogw.at[:, pl.ds(y * ob, ob)]
+        return remote(ref, ref, v_send.at[k - 1], v_recv.at[k - 1], dev(xh, lax.rem(y + k, NY), xl, z))
+
+    def v_arrival(k):
+        ref = ogw.at[:, pl.ds(lax.rem(y + NY - k, NY) * ob, ob)]
+        return remote(ref, ref, v_send.at[k - 1], v_recv.at[k - 1], dev(xh, lax.rem(y + k, NY), xl, z))
 
     def strip(h, y_):
         return ogi.at[:, h, pl.ds(y_ * quarter, quarter)]
@@ -236,6 +245,7 @@
     hops = NZ // 2
     waiting = []
     next_product = 0
+    w_start()
     for item in range(LOOK):
         ring_start(item, 1)
 
@@ -258,7 +268,9 @@
             for k in range(1, NY):
                 src = ogy.at[pl.ds(lax.rem(y + NY - k, NY) * ob, ob)]
                 remote(src, src, y_send.at[k - 1], y_recv.at[k - 1], dev(xh, lax.rem(y + k, NY), xl, z)).wait_recv()
-            w_start()
+            w_wait()
+            for k in range(1, NY):
+                v_copy(k).start()
             for k in range(1, NZ):
                 z_copy(k).start()
             z_local.start()
@@ -275,7 +287,8 @@
                 b_copy(1, k).start()
         while next_product < len(prods) and due(prods[next_product][0], hops) <= step:
             if next_product == 0:
-                w_wait()
+                for k in range(1, NY):
+                    v_arrival(k).wait_recv()
             if next_product == n_chunks:
                 for which in (0, 1):
                     for k in range(1, NY):
@@ -292,6 +305,8 @@
     for copy in y_copies + ring_copies:
         copy.wait_send()
     w_wait_send()
+    for k in range(1, NY):
+        v_copy(k).wait_send()
     for k in range(1, NZ):
         z_copy(k).wait_send()
     h_copy.wait_send()
@@ -336,6 +351,8 @@
             dma((NY - 1,)),
             dma((XH,)),
             dma((XL,)),
+            dma((NY - 1,)),
+            dma((NY - 1,)),
             dma((NZ - 1,)),
             dma((NZ - 1,)),
             dma,

time: 138 us -> 138 us (level)
  no operation moved by 1% of the time
where the time goes in v3:
time: 138 us
  Pallas kernels  132 us (96%)
  other arithmetic  4.28 us (3%)
    pallas_call x1, Pallas kernels, products(): pl.pallas_call(kernel, out_shape=(jax.ShapeDtypeStruct((d, f), jnp.float3...  132 us
    convert_element_type x1, other arithmetic, per_device(): (old - 0.001 * first_hat / (jnp.sqrt(second_hat) + 1e-08) - 0.0001 * old)...  4.28 us

profile of v3, /device:TPU:4, one launch (start us, length us, event | category | flops | bytes accessed | tf_op | source)
XLA Modules:
  0.0 137.7 jit_solution(1707010042925630809)
XLA Ops:
  0.6 0.0 copy-start.2
  0.6 0.0 copy-start.1
  0.7 0.0 copy-start
  0.7 131.9 %shard_map.84 = (f32[1536,256]{1,0:T(8,128)}, bf16[192,1536]{1,0:T(8,128)(2,1)}) custom-call(bf16[192,1536]{1,0:T(8,128)(2,1)} %tokens.1, bf16[384,256]{1,0:T(8,128)(2,1)} %og.1, bf16[1536,256]{1,0:T(8,128)(2,1)} %weight.1), custom_call_target="tpu_custom_call" | custom-call | flops 4831838208 | bytes 8388608 | tf_op jit(solution)/shard_map/pallas_call | solution.py:329
  132.6 0.0 copy-done.2
  132.6 0.0 copy-done.1
  132.6 0.0 copy-done
  132.6 0.0 copy-start.3
  132.6 4.3 %fusion.1 = (bf16[1536,256]{1,0:T(8,128)(2,1)}, f32[1536,256]{1,0:T(8,128)}, f32[1536,256]{1,0:T(8,128)}) fusion(bf16[1536,256]{1,0:T(8,128)(2,1)S(1)} %copy-done.2, f32[1536,256]{1,0:T(8,128)} %get-tuple-element.7, f32[1536,256]{1,0:T(8,128)S(1)} %copy-done, f32[1536,256]{1,0:T(8,128)S(1)} %copy-done.1), kind=kLoop, calls=%fused_computation.4 | loop fusion | flops 6291456 | bytes 9437184 | tf_op jit(solution)/shard_map/convert_element_type | solution.py:380
  136.9 0.0 copy-done.3
  136.9 0.8 copy.10
Async XLA Ops:
  0.6 132.0 %copy-start.2 = (bf16[1536,256]{1,0:T(8,128)(2,1)S(1)}, bf16[1536,256]{1,0:T(8,128)(2,1)}, u32[]{:S(2)}) copy-start(bf16[1536,256]{1,0:T(8,128)(2,1)} %weight.1) | copy-start | bytes 2359300
  0.6 132.0 %copy-start.1 = (f32[1536,256]{1,0:T(8,128)S(1)}, f32[1536,256]{1,0:T(8,128)}, u32[]{:S(2)}) copy-start(f32[1536,256]{1,0:T(8,128)} %param.9) | copy-start | bytes 4718596
  0.7 132.0 %copy-start = (f32[1536,256]{1,0:T(8,128)S(1)}, f32[1536,256]{1,0:T(8,128)}, u32[]{:S(2)}) copy-start(f32[1536,256]{1,0:T(8,128)} %param.8) | copy-start | bytes 4718596
  132.6 4.3 %copy-start.3 = (bf16[192,1536]{1,0:T(8,128)(2,1)S(1)}, bf16[192,1536]{1,0:T(8,128)(2,1)}, u32[]{:S(2)}) copy-start(bf16[192,1536]{1,0:T(8,128)(2,1)} %get-tuple-element.15) | copy-start | bytes 1769476

commit v4 on v3

--- a/solution.py
+++ b/solution.py
@@ -12,7 +12,7 @@
 XH, XL, NY, NZ = 2, 2, 4, 8
 LOOK = 4
 TOKEN_CHUNKS = (384, 384, 384, 384)
-WEIGHT_CHUNKS = (384, 384, 384, 256, 128)
+WEIGHT_CHUNKS = (512, 384, 384, 128, 128)
 LAST = 128
 PACE = 1
 DRAIN = 0

time: 138 us -> 138 us (level)
  no operation moved by 1% of the time
where the time goes in v4:
time: 138 us
  Pallas kernels  132 us (96%)
  other arithmetic  4.28 us (3%)
    pallas_call x1, Pallas kernels, products(): pl.pallas_call(kernel, out_shape=(jax.ShapeDtypeStruct((d, f), jnp.float3...  132 us
    convert_element_type x1, other arithmetic, per_device(): (old - 0.001 * first_hat / (jnp.sqrt(second_hat) + 1e-08) - 0.0001 * old)...  4.28 us

profile of v4, /device:TPU:4, one launch (start us, length us, event | category | flops | bytes accessed | tf_op | source)
XLA Modules:
  0.0 138.1 jit_solution(95459208359912482)
XLA Ops:
  0.6 0.0 copy-start.2
  0.6 0.0 copy-start.1
  0.7 0.0 copy-start
  0.7 132.3 %shard_map.84 = (f32[1536,256]{1,0:T(8,128)}, bf16[192,1536]{1,0:T(8,128)(2,1)}) custom-call(bf16[192,1536]{1,0:T(8,128)(2,1)} %tokens.1, bf16[384,256]{1,0:T(8,128)(2,1)} %og.1, bf16[1536,256]{1,0:T(8,128)(2,1)} %weight.1), custom_call_target="tpu_custom_call" | custom-call | flops 4831838208 | bytes 8388608 | tf_op jit(solution)/shard_map/pallas_call | solution.py:329
  132.9 0.0 copy-done.2
  132.9 0.0 copy-done.1
  132.9 0.0 copy-done
  133.0 0.0 copy-start.3
  133.0 4.3 %fusion.1 = (bf16[1536,256]{1,0:T(8,128)(2,1)}, f32[1536,256]{1,0:T(8,128)}, f32[1536,256]{1,0:T(8,128)}) fusion(bf16[1536,256]{1,0:T(8,128)(2,1)S(1)} %copy-done.2, f32[1536,256]{1,0:T(8,128)} %get-tuple-element.7, f32[1536,256]{1,0:T(8,128)S(1)} %copy-done, f32[1536,256]{1,0:T(8,128)S(1)} %copy-done.1), kind=kLoop, calls=%fused_computation.4 | loop fusion | flops 6291456 | bytes 9437184 | tf_op jit(solution)/shard_map/convert_element_type | solution.py:380
  137.2 0.0 copy-done.3
  137.3 0.8 copy.10
Async XLA Ops:
  0.6 132.3 %copy-start.2 = (bf16[1536,256]{1,0:T(8,128)(2,1)S(1)}, bf16[1536,256]{1,0:T(8,128)(2,1)}, u32[]{:S(2)}) copy-start(bf16[1536,256]{1,0:T(8,128)(2,1)} %weight.1) | copy-start | bytes 2359300
  0.6 132.3 %copy-start.1 = (f32[1536,256]{1,0:T(8,128)S(1)}, f32[1536,256]{1,0:T(8,128)}, u32[]{:S(2)}) copy-start(f32[1536,256]{1,0:T(8,128)} %param.9) | copy-start | bytes 4718596
  0.7 132.3 %copy-start = (f32[1536,256]{1,0:T(8,128)S(1)}, f32[1536,256]{1,0:T(8,128)}, u32[]{:S(2)}) copy-start(f32[1536,256]{1,0:T(8,128)} %param.8) | copy-start | bytes 4718596
  133.0 4.3 %copy-start.3 = (bf16[192,1536]{1,0:T(8,128)(2,1)S(1)}, bf16[192,1536]{1,0:T(8,128)(2,1)}, u32[]{:S(2)}) copy-start(bf16[192,1536]{1,0:T(8,128)(2,1)} %get-tuple-element.15) | copy-start | bytes 1769476
